TPU v7x, 256 devices: a whole 4x4x8 slice. The times are simulated.
256 devices in a mesh: grp: 8 (over x, core), row: 32 (over z, y).
Axes of the slice: x: 4, y: 4, z: 8, core: 2. Of those that a mesh axis runs over, the one named last changes fastest.
Arguments:
- embeddings: float32 [131072, 4096], P(('grp', 'row')), may hold values from -225 to 225, as said below
- sketch: float32 [4096, 128], replicated, may hold values from -6 to 6
Outputs:
- row_basis: float32 [131072, 128], P(('grp', 'row'))
- column_factor: float32 [4096, 128], P(('grp', 'row'))
- first_factor: float32 [4096, 128], P(('grp', 'row'))
Inputs may be any that keep to these rules, and one draw needn't show every extreme that they name: real-valued document embeddings.
All inputs are finite; a program needn't handle non-finite values.
Results may differ from a plain program's by a relative error of at most 0.000073.
Values sent between devices are 32-bit elements; how exact they have to be, the bound alone decides.
A program may use at most 64 MiB of HBM per device.

v0:
```python
import math

import jax
import jax.numpy as jnp
from jax import lax
from jax.sharding import PartitionSpec as P


def product(left, right):
    return jnp.dot(left, right, precision=lax.Precision.HIGHEST, preferred_element_type=jnp.float32)


def local_gram(tall_block):
    return product(tall_block.T, tall_block)


def apply_inverse(lower_factor, tall_block):
    return jax.scipy.linalg.solve_triangular(lower_factor, tall_block.T, lower=True).T


def per_device(embeddings, sketch):
    devices_all = lax.axis_size(("grp", "row"))
    root_rows = math.sqrt(embeddings.shape[0] * devices_all)
    first_image = product(embeddings, sketch)
    gram_one = lax.psum(local_gram(first_image), ("grp", "row"))
    basis_one = apply_inverse(jnp.linalg.cholesky(gram_one), first_image)
    back_product = lax.psum(product(embeddings.T, basis_one), ("grp", "row"))
    slab_rows = embeddings.shape[1] // devices_all
    position = lax.axis_index(("grp", "row")) * slab_rows
    first_slab = lax.dynamic_slice_in_dim(back_product, position, slab_rows, 0) / root_rows
    second = product(embeddings, back_product)
    gram_two = lax.psum(local_gram(second), ("grp", "row"))
    lower_two = jnp.linalg.cholesky(gram_two)
    basis_two = apply_inverse(lower_two, second)
    whole_factor = lax.psum(product(embeddings.T, basis_two), ("grp", "row"))
    slab_part = lax.dynamic_slice_in_dim(whole_factor, position, slab_rows, 0)
    return (basis_two * root_rows, slab_part / root_rows, first_slab)


def solution(mesh):
    placed = (P(("grp", "row"), None), P())
    return jax.shard_map(
        per_device,
        mesh=mesh,
        in_specs=placed,
        out_specs=(P(("grp", "row"), None), P(("grp", "row"), None), P(("grp", "row"), None)),
        check_vma=False,
    )
```

profile of v0, /device:TPU:1, one launch (start us, length us, event | category | flops | bytes accessed | tf_op | source)
XLA Modules:
  0.0 1098.9 jit_solution(6142291724762245244)
XLA Ops:
  7.2 0.0 copy-start
  7.2 0.0 all-reduce.5.cloned.1.call-start
  7.2 1.5 copy-done
  8.8 9.1 fusion.11
  17.9 1.2 fusion.12
  19.1 0.0 all-reduce.5.cloned.1.call-update
  19.1 0.2 all-reduce.7.cloned.1.call-start
  19.4 241.8 %all-reduce.5.cloned.1.call-done = f32[128,128]{0,1:T(8,128)} async-done(((f32[128,128]{0,1:T(8,128)}), f32[128,128]{0,1:T(8,128)}) %all-reduce.5.cloned.1.call-update) | async-done | bytes 65552 | tf_op jit(solution)/shard_map/psum | solution.py:25
  261.1 0.9 copy.6
  262.1 0.9 fusion.8
  262.9 11.7 %cholesky.44 = f32[128,128]{1,0:T(8,128)S(1)} custom-call(f32[128,128]{1,0:T(8,128)S(1)} %fusion.8), custom_call_target="Cholesky" | custom-call | tf_op jit(solution)/shard_map/jit(cholesky)/cholesky | solution.py:26
  274.7 0.6 compare_reduce_fusion.1
  275.3 0.7 fusion.2
  276.0 9.8 custom-call.6
  285.8 0.4 fusion
  286.2 8.2 convolution_bitcast_fusion.1
  294.4 0.0 all-reduce.7.cloned.1.call-update
  294.4 0.3 all-reduce.9.cloned.1.call-start
  294.7 255.7 %all-reduce.7.cloned.1.call-done = f32[4096,128]{0,1:T(8,128)} async-done(((f32[4096,128]{0,1:T(8,128)}), f32[4096,128]{0,1:T(8,128)}) %all-reduce.7.cloned.1.call-update) | async-done | bytes 2097168 | tf_op jit(solution)/shard_map/psum | solution.py:27
  550.4 11.6 %fusion.13 = f32[128,512]{1,0:T(8,128)S(1)} fusion(f32[4096,128]{0,1:T(8,128)} %all-reduce.7.cloned.1.call-done, f32[512,4096]{1,0:T(8,128)} %param.5), kind=kOutput, calls=%fused_computation.27 | convolution fusion | flops 3221225472 | bytes 10747904 | tf_op jit(solution)/shard_map/dot_general | solution.py:10
  562.0 1.0 fusion.14
  563.1 0.0 all-reduce.9.cloned.1.call-update
  563.1 0.0 all-reduce.11.cloned.1.call-start
  563.1 238.2 %all-reduce.9.cloned.1.call-done = f32[128,128]{0,1:T(8,128)} async-done(((f32[128,128]{0,1:T(8,128)}), f32[128,128]{0,1:T(8,128)}) %all-reduce.9.cloned.1.call-update) | async-done | bytes 65552 | tf_op jit(solution)/shard_map/psum | solution.py:32
  801.3 0.9 copy.8
  802.3 0.9 fusion.6
  803.1 11.7 %cholesky.55 = f32[128,128]{1,0:T(8,128)S(1)} custom-call(f32[128,128]{1,0:T(8,128)S(1)} %fusion.6), custom_call_target="Cholesky" | custom-call | tf_op jit(solution)/shard_map/jit(cholesky)/cholesky | solution.py:33
  814.9 0.6 compare_reduce_fusion
  815.5 0.7 fusion.3
  816.2 9.8 custom-call.7
  826.0 0.4 fusion.4
  826.4 8.2 convolution_bitcast_fusion
  834.6 0.0 all-reduce.11.cloned.1.call-update
  834.6 0.9 dynamic-slice_multiply_fusion
  835.6 0.7 copy.11
  836.3 0.8 copy.9
  837.1 253.7 %all-reduce.11.cloned.1.call-done = f32[4096,128]{0,1:T(8,128)} async-done(((f32[4096,128]{0,1:T(8,128)}), f32[4096,128]{0,1:T(8,128)}) %all-reduce.11.cloned.1.call-update) | async-done | bytes 2097168 | tf_op jit(solution)/shard_map/psum | solution.py:35
  1090.8 0.9 dynamic-slice_multiply_fusion.1
  1091.7 0.7 copy.10
  (3 shorter events, 0.1 us)
Async XLA Ops:
  7.2 1.6 copy-start
  7.2 254.0 %all-reduce.5.cloned.1.call-start = ((), (), s32[]{:S(2)}) async-start(), calls=%async_computation | async-start | bytes 131072 | tf_op jit(solution)/shard_map/psum | solution.py:25
  19.1 531.3 %all-reduce.7.cloned.1.call-start = ((), (), s32[]{:S(2)}) async-start(), calls=%async_computation.1 | async-start | bytes 4194304 | tf_op jit(solution)/shard_map/psum | solution.py:27
  294.4 506.9 %all-reduce.9.cloned.1.call-start = ((), (), s32[]{:S(2)}) async-start(), calls=%async_computation.2 | async-start | bytes 131072 | tf_op jit(solution)/shard_map/psum | solution.py:32
  563.1 527.7 %all-reduce.11.cloned.1.call-start = ((), (), s32[]{:S(2)}) async-start(), calls=%async_computation.3 | async-start | bytes 4194304 | tf_op jit(solution)/shard_map/psum | solution.py:35
Sparse Core Ops, SparseCore 0:
  19.2 241.8 all-reduce.4
  294.5 255.8 all-reduce.6
  563.2 238.0 all-reduce.8
  834.8 256.0 all-reduce.10
where the time goes:
time: 1100 us
  waiting for transfers between devices  989 us (90%)
  other arithmetic  49.3 us (4%)
  matrix products  40.2 us (4%)
  between operations  13.9 us (1%)
    psum x1, waiting for transfers between devices, per_device(): back_product = lax.psum(product(embeddings.T, basis_one), ('grp', 'row'))  256 us
    psum x1, waiting for transfers between devices, per_device(): whole_factor = lax.psum(product(embeddings.T, basis_two), ('grp', 'row'))  254 us
    psum x1, waiting for transfers between devices, per_device(): gram_one = lax.psum(local_gram(first_image), ('grp', 'row'))  242 us
    psum x1, waiting for transfers between devices, per_device(): gram_two = lax.psum(local_gram(second), ('grp', 'row'))  238 us
    dot_general x6, matrix products, product(): jnp.dot(left, right, precision=lax.Precision.HIGHEST, preferred_element_t...  39.4 us
  transfers between devices with their start and end apart: 4, of which 4 were waited for; matrix products, arithmetic and copies ran while one was open for 0% of the time, Pallas kernels for 0%

commit v1 on v0

v1 whole, which is shorter than its diff:
```python
import math

import jax
import jax.numpy as jnp
from jax import lax
from jax.experimental import pallas as pl
from jax.experimental.pallas import tpu as pltpu
from jax.sharding import PartitionSpec as P

MESH = pl.DeviceIdType.MESH
HIGHEST = lax.Precision.HIGHEST
F32, BF16 = jnp.float32, jnp.bfloat16
K = 128
NX, NY, NZ = 4, 4, 8
SLAB = 16
BLOCK = NY * NZ * SLAB
NBLOCK = 2 * NX


def split(value):
    high = value.astype(BF16)
    return high, (value - high.astype(F32)).astype(BF16)


def dot(left, right):
    return jnp.dot(left, right, preferred_element_type=F32)


def lane_broadcast(value, lane):
    return jnp.broadcast_to(value[:, lane : lane + 1], value.shape)


def row_broadcast(value, row):
    return jnp.broadcast_to(value[row : row + 1, :], value.shape)


def cholesky_inverse(tiles):
    lane = lax.broadcasted_iota(jnp.int32, (8, K), 1)
    sub = lax.broadcasted_iota(jnp.int32, (8, K), 0)
    tiles = list(tiles)
    for b in range(len(tiles)):
        cur = tiles[b]
        inside = (lane >= 8 * b) & (lane < 8 * b + 8)
        cols = [lane_broadcast(cur, 8 * b + k) for k in range(8)]
        low = {(i, k): row_broadcast(cols[k], i) for k in range(8) for i in range(k, 8)}
        rows = [
            jnp.where(inside, jnp.where(lane == 8 * b + i, 1.0, 0.0), row_broadcast(cur, i))
            for i in range(8)
        ]
        inv = []
        for k in range(8):
            inv.append(lax.rsqrt(low[k, k]))
            for i in range(k + 1, 8):
                low[i, k] = low[i, k] * inv[k]
            for i in range(k + 1, 8):
                for m in range(k + 1, i + 1):
                    low[i, m] = low[i, m] - low[i, k] * low[m, k]
        for k in range(8):
            rows[k] = rows[k] * inv[k]
            for i in range(k + 1, 8):
                rows[i] = rows[i] - low[i, k] * rows[k]
        for t in range(b + 1, len(tiles)):
            col = [lane_broadcast(tiles[t], 8 * b + k) for k in range(8)]
            acc = jnp.where(inside, 0.0, tiles[t])
            for k in range(8):
                col[k] = col[k] * inv[k]
                for m in range(k + 1, 8):
                    col[m] = col[m] - col[k] * low[m, k]
                acc = acc - col[k] * rows[k]
            tiles[t] = acc
        new = rows[0]
        for i in range(1, 8):
            new = jnp.where(sub == i, rows[i], new)
        tiles[b] = jnp.where(lane <= sub + 8 * b, new, 0.0)
    return tiles


def times_transposed(value, inverse):
    left_high, left_low = split(value)
    right_high, right_low = split(inverse.T)
    return dot(left_high, right_high) + (dot(left_high, right_low) + dot(left_low, right_high))


def kernel(
    x_hbm, s_hbm, basis_ref, column_ref, first_ref,
    x_in, s_in, x_high, x_low, s_pair, total, wide, tall,
    zfull,
    core_out, core_in, own, half, in1, part2, in2, part3, in3,
    gram, gram_in, gram_mid, gram_core, gram_z, gram_all, inverse,
    load_sem, core_send, core_recv, s1, r1, s2, r2, s3, r3,
    az_s, az_r, a2_s, a2_r, a1_s, a1_r, ac_s, ac_r,
    gx_s, gx_r, gc_s, gc_r, gz_s, gz_r, ga_s, ga_r,
):
    grp, row = lax.axis_index("grp"), lax.axis_index("row")
    x, core = grp // 2, grp % 2
    z, y = row // NY, row % NY
    other = 1 - core
    swap = core == 1
    first = jnp.where(swap, y, x)
    second = jnp.where(swap, x, y)
    place = first * 4 + second

    def device(px, pc, pz, py):
        return (px * 2 + pc, pz * NY + py)

    def along_first(step):
        at = lax.rem(first + step, 4)
        return at, device(jnp.where(swap, x, at), core, z, jnp.where(swap, at, y))

    def along_second(step):
        at = lax.rem(second + step, 4)
        return at, device(jnp.where(swap, at, x), core, z, jnp.where(swap, y, at))

    def along_z(step):
        at = lax.rem(z + step, NZ)
        return at, device(x, core, at, y)

    plane = [(i, j) for i in (2, 1, 3, 0) for j in (2, 1, 3, 0) if i or j]
    near = (2, 1, 3)
    ring = (4, 3, 5, 2, 6, 1, 7)

    def in_plane(step):
        px, py = lax.rem(x + step[0], 4), lax.rem(y + step[1], 4)
        return px * 4 + py, device(px, core, z, py)

    partner = device(x, other, z, y)

    def remote(src, dst, send, recv, to):
        return pltpu.make_async_remote_copy(
            src_ref=src, dst_ref=dst, send_sem=send, recv_sem=recv, device_id=to, device_id_type=MESH
        )

    barrier = pltpu.get_barrier_semaphore()
    peers = [partner] + [in_plane(s)[1] for s in plane] + [along_z(s)[1] for s in ring]
    for peer in peers:
        pl.semaphore_signal(barrier, inc=1, device_id=peer, device_id_type=MESH)

    loads = []
    for j in range(NBLOCK):
        cols = pl.ds(BLOCK * j, BLOCK)
        pair = (
            pltpu.make_async_copy(x_hbm.at[:, cols], x_in.at[j], load_sem.at[2 * j]),
            pltpu.make_async_copy(s_hbm.at[cols], s_in.at[j], load_sem.at[2 * j + 1]),
        )
        for copy in pair:
            copy.start()
        loads.append(pair)

    def start(copies):
        for copy in copies:
            copy.start()
        return copies

    def wait(copies):
        for copy in copies:
            copy.wait()

    def gram_start(g, block):
        gram[g] = dot_highest(block)
        return start([
            remote(gram.at[g, in_plane(s)[0]], gram_in.at[g, k], gx_s.at[g, k], gx_r.at[g, k], in_plane(s)[1])
            for k, s in enumerate(plane)
        ])

    def dot_highest(block):
        product = jnp.dot(block.T, block, precision=HIGHEST, preferred_element_type=F32)
        return product.reshape(16, 8, K)

    def gram_core_step(g, copies):
        wait(copies)
        tile = gram[g, x * 4 + y]
        for k in range(len(plane)):
            tile = tile + gram_in[g, k]
        gram_mid[g] = tile
        return start([remote(gram_mid.at[g], gram_core.at[g], gc_s.at[g], gc_r.at[g], partner)])

    def gram_z_step(g, copies):
        wait(copies)
        gram_z[g, z] = gram_mid[g] + gram_core[g]
        return start([
            remote(gram_z.at[g, z], gram_z.at[g, z], gz_s.at[g, k], gz_r.at[g, k], along_z(s)[1])
            for k, s in enumerate(ring)
        ])

    def gram_back_step(g, copies):
        wait(copies)
        tile = gram_z[g, 0]
        for k in range(1, NZ):
            tile = tile + gram_z[g, k]
        at = x * 4 + y
        gram_all[g, at] = tile
        return start([
            remote(gram_all.at[g, at], gram_all.at[g, at], ga_s.at[g, k], ga_r.at[g, k], in_plane(s)[1])
            for k, s in enumerate(plane)
        ])

    def gram_finish(g, copies):
        wait(copies)
        tiles = cholesky_inverse([gram_all[g, t] for t in range(16)])
        for t in range(16):
            inverse[g, pl.ds(8 * t, 8), :] = tiles[t]

    def transposed_block(j):
        part = dot(wide[...], x_high[j])
        part = part[0:K] + part[K : 2 * K] + dot(wide[0:K, :], x_low[j])
        return part.T.reshape(NZ, NY, SLAB, K)

    def prepare(block):
        high, low = split(block.T)
        wide[0:K, :] = high
        wide[K : 2 * K, :] = low

    def core_start(n):
        copies = []
        for px in range(NX):
            core_out[n, px] = transposed_block(px * 2 + other)
            copies += start([remote(core_out.at[n, px], core_in.at[n, px], core_send.at[n, px], core_recv.at[n, px], partner)])
        for px in range(NX):
            own[px] = transposed_block(px * 2 + core)
        return copies

    def first_step(n, copies):
        for px in range(NX):
            copies[px].wait()
            for py in range(NY):
                at = jnp.where(swap, py * 4 + px, px * 4 + py)
                half[n, at] = own[px, :, py] + core_in[n, px, :, py]
        return start([
            remote(half.at[n, pl.ds(along_first(s)[0] * 4, 4)], in1.at[n, k], s1.at[n, k], r1.at[n, k], along_first(s)[1])
            for k, s in enumerate(near)
        ])

    def second_step(n, copies):
        wait(copies)
        for i in range(4):
            part2[n, i] = (half[n, first * 4 + i] + in1[n, 0, i]) + (in1[n, 1, i] + in1[n, 2, i])
        return start([
            remote(part2.at[n, along_second(s)[0]], in2.at[n, k], s2.at[n, k], r2.at[n, k], along_second(s)[1])
            for k, s in enumerate(near)
        ])

    def z_step(n, copies):
        wait(copies)
        part3[n] = (part2[n, second] + in2[n, 0]) + (in2[n, 1] + in2[n, 2])
        return start([
            remote(part3.at[n, along_z(s)[0]], in3.at[n, k], s3.at[n, k], r3.at[n, k], along_z(s)[1])
            for k, s in enumerate(ring)
        ])

    def slab_of(n, copies):
        wait(copies)
        slab = part3[n, z]
        for k in range(len(ring)):
            slab = slab + in3[n, k]
        return slab

    total[...] = jnp.zeros_like(total)
    for j in range(NBLOCK):
        for copy in loads[j]:
            copy.wait()
        s_high, s_low = split(s_in[j])
        s_pair[j, :, 0:K] = s_high
        s_pair[j, :, K : 2 * K] = s_low
        high, low = split(x_in[j])
        x_high[j] = high
        x_low[j] = low
        part = dot(high, s_pair[j])
        total[...] += part[:, 0:K] + part[:, K : 2 * K] + dot(low, s_high)
    image = total[...]
    prepare(image)
    pl.semaphore_wait(barrier, len(peers))

    gram_copies = gram_start(0, image)
    copies = core_start(0)
    copies = first_step(0, copies)
    gram_copies = gram_core_step(0, gram_copies)
    gram_copies = gram_z_step(0, gram_copies)
    copies = second_step(0, copies)
    gram_copies = gram_back_step(0, gram_copies)
    copies = z_step(0, copies)
    slab = slab_of(0, copies)

    zfull[core, place, z] = slab
    copies = start([
        remote(zfull.at[core, place, z], zfull.at[core, place, z], az_s.at[k], az_r.at[k], along_z(s)[1])
        for k, s in enumerate(ring)
    ])
    wait(copies)
    copies = start([
        remote(zfull.at[core, place], zfull.at[core, place], a2_s.at[k], a2_r.at[k], along_second(s)[1])
        for k, s in enumerate(near)
    ])
    wait(copies)
    mine = pl.ds(first * 4, 4)
    copies = start([
        remote(zfull.at[core, mine], zfull.at[core, mine], a1_s.at[k], a1_r.at[k], along_first(s)[1])
        for k, s in enumerate(near)
    ])
    gram_finish(0, gram_copies)
    root_rows = math.sqrt(x_hbm.shape[0] * 256)
    first_ref[...] = times_transposed(slab, inverse[0]) / root_rows
    wait(copies)
    copies = start([remote(zfull.at[core], zfull.at[core], ac_s.at[0], ac_r.at[0], partner)])

    def image_of(half_core, px):
        for py in range(NY):
            at = jnp.where(half_core == 1, py * 4 + px, px * 4 + py)
            high, low = split(zfull[half_core, at])
            tall[px, :, py, :, 0:K] = high
            tall[px, :, py, :, K : 2 * K] = low
        right = tall[px].reshape(BLOCK, 2 * K)
        part = dot(x_high[px * 2 + half_core], right)
        return part[:, 0:K] + part[:, K : 2 * K] + dot(x_low[px * 2 + half_core], right[:, 0:K])

    total[...] = image_of(core, 0)
    for px in range(1, NX):
        total[...] += image_of(core, px)
    wait(copies)
    for px in range(NX):
        total[...] += image_of(other, px)
    total[...] = times_transposed(total[...], inverse[0])
    image = total[...]
    prepare(image)

    gram_copies = gram_start(1, image)
    copies = core_start(1)
    copies = first_step(1, copies)
    gram_copies = gram_core_step(1, gram_copies)
    gram_copies = gram_z_step(1, gram_copies)
    copies = second_step(1, copies)
    gram_copies = gram_back_step(1, gram_copies)
    copies = z_step(1, copies)
    gram_finish(1, gram_copies)
    basis_ref[...] = times_transposed(total[...], inverse[1]) * root_rows
    slab = slab_of(1, copies)
    column_ref[...] = times_transposed(slab, inverse[1]) / root_rows


def per_device(embeddings, sketch):
    rows = embeddings.shape[0]
    dma = pltpu.SemaphoreType.DMA
    vmem = pltpu.VMEM
    scratch = [
        vmem((NBLOCK, rows, BLOCK), F32),
        vmem((NBLOCK, BLOCK, K), F32),
        vmem((NBLOCK, rows, BLOCK), BF16),
        vmem((NBLOCK, rows, BLOCK), BF16),
        vmem((NBLOCK, BLOCK, 2 * K), BF16),
        vmem((rows, K), F32),
        vmem((2 * K, rows), BF16),
        vmem((NX, NZ, NY, SLAB, 2 * K), BF16),
        vmem((2, 16, NZ, SLAB, K), F32),
        vmem((2, NX, NZ, NY, SLAB, K), F32),
        vmem((2, NX, NZ, NY, SLAB, K), F32),
        vmem((NX, NZ, NY, SLAB, K), F32),
        vmem((2, 16, NZ, SLAB, K), F32),
        vmem((2, 3, 4, NZ, SLAB, K), F32),
        vmem((2, 4, NZ, SLAB, K), F32),
        vmem((2, 3, NZ, SLAB, K), F32),
        vmem((2, NZ, SLAB, K), F32),
        vmem((2, 7, SLAB, K), F32),
        vmem((2, 16, 8, K), F32),
        vmem((2, 15, 8, K), F32),
        vmem((2, 8, K), F32),
        vmem((2, 8, K), F32),
        vmem((2, NZ, 8, K), F32),
        vmem((2, 16, 8, K), F32),
        vmem((2, K, K), F32),
        dma((2 * NBLOCK,)),
        dma((2, NX)), dma((2, NX)),
        dma((2, 3)), dma((2, 3)),
        dma((2, 3)), dma((2, 3)),
        dma((2, 7)), dma((2, 7)),
        dma((7,)), dma((7,)),
        dma((3,)), dma((3,)),
        dma((3,)), dma((3,)),
        dma((1,)), dma((1,)),
        dma((2, 15)), dma((2, 15)),
        dma((2,)), dma((2,)),
        dma((2, 7)), dma((2, 7)),
        dma((2, 15)), dma((2, 15)),
    ]
    anywhere = pl.BlockSpec(memory_space=pl.ANY)
    return pl.pallas_call(
        kernel,
        name="subspace_iteration",
        out_shape=(
            jax.ShapeDtypeStruct((rows, K), F32),
            jax.ShapeDtypeStruct((SLAB, K), F32),
            jax.ShapeDtypeStruct((SLAB, K), F32),
        ),
        in_specs=[anywhere, anywhere],
        out_specs=[pl.BlockSpec(memory_space=pltpu.VMEM)] * 3,
        scratch_shapes=scratch,
        compiler_params=pltpu.CompilerParams(
            collective_id=0, has_side_effects=True, vmem_limit_bytes=48 * 2**20
        ),
        cost_estimate=pl.CostEstimate(
            flops=4 * 2 * rows * embeddings.shape[1] * K, bytes_accessed=11 * 2**20, transcendentals=0
        ),
    )(embeddings, sketch)


def solution(mesh):
    rows = P(("grp", "row"), None)
    return jax.shard_map(
        per_device, mesh=mesh, in_specs=(rows, P()), out_specs=(rows, rows, rows), check_vma=False
    )
```

time: 1100 us -> 87.3 us (0.08)
  waiting for transfers between devices: 989 us -> 0 us
  Pallas kernels: 0 us -> 83 us
  other arithmetic: 49.3 us -> 0 us
  matrix products: 40.2 us -> 0 us
  between operations: 13.9 us -> 0.65 us
    psum x4 -> x0, waiting for transfers between devices: 989 us -> none  [the longest x1 256 us: per_device(): back_product = lax.psum(product(embeddings.T, basis_one), ('grp', 'row'))]
    pallas_call x0 -> x1, Pallas kernels: none -> 83 us  [per_device(): pl.pallas_call(kernel, name='subspace_iteration', out_shape=(jax.ShapeDty...]
    another operation x10 -> x0, other arithmetic: 45.7 us -> none  [the longest x4 20.9 us: apply_inverse(): jax.scipy.linalg.solve_triangular(lower_factor, tall_block.T, lower=True)]
    dot_general x6 -> x0, matrix products: 39.4 us -> none  [product(): jnp.dot(left, right, precision=lax.Precision.HIGHEST, preferred_element_t...]
  transfers between devices with their start and end apart: 4 -> 0, of which waited for: 4 -> 0; matrix products, arithmetic and copies ran while one was open for 0% -> 0% of each run, Pallas kernels for 0% -> 0%
where the time goes in v1:
time: 87.3 us; the launch traced here: 87.2 us
  Pallas kernels  83 us (95%)
  local copies, waits for them, and re-layouts  3.49 us (4%)
    pallas_call x1, Pallas kernels, per_device(): pl.pallas_call(kernel, name='subspace_iteration', out_shape=(jax.ShapeDty...  83 us
    unnamed x5, local copies, waits for them, and re-layouts  3.49 us

profile of v1, /device:TPU:1, one launch (start us, length us, event | category | flops | bytes accessed | tf_op | source)
XLA Modules:
  0.0 87.2 jit_solution(4912903863257617334)
XLA Ops:
  0.6 0.0 copy-start
  0.6 1.6 %copy-done = f32[4096,128]{1,0:T(8,128)S(1)} copy-done((f32[4096,128]{1,0:T(8,128)S(1)}, f32[4096,128]{1,0:T(8,128)}, u32[]{:S(2)}) %copy-start) | copy-done | bytes 2097176
  2.2 83.0 %subspace_iteration.1 = (f32[512,128]{1,0:T(8,128)S(1)}, f32[16,128]{1,0:T(8,128)S(1)}, f32[16,128]{1,0:T(8,128)S(1)}) custom-call(f32[512,4096]{1,0:T(8,128)} %x_hbm.1, f32[4096,128]{1,0:T(8,128)S(1)} %copy-done), custom_call_target="tpu_custom_call" | custom-call | flops 2147483648 | bytes 11534336 | tf_op jit(solution)/shard_map/subspace_iteration/pallas_call | solution.py:384
  85.3 0.7 copy.8
  86.0 0.6 copy.9
  86.6 0.6 copy.10
Async XLA Ops:
  0.6 1.6 %copy-start = (f32[4096,128]{1,0:T(8,128)S(1)}, f32[4096,128]{1,0:T(8,128)}, u32[]{:S(2)}) copy-start(f32[4096,128]{1,0:T(8,128)} %s_hbm.1) | copy-start | bytes 6291460

commit v2 on v1

v2 whole, which is shorter than its diff:
```python
import math

import jax
import jax.numpy as jnp
from jax import lax
from jax.experimental import pallas as pl
from jax.experimental.pallas import tpu as pltpu
from jax.sharding import PartitionSpec as P

MESH = pl.DeviceIdType.MESH
HIGHEST = lax.Precision.HIGHEST
F32, BF16 = jnp.float32, jnp.bfloat16
K = 128
NX, NY, NZ = 4, 4, 8
SLAB = 16
BLOCK = NY * NZ * SLAB
NBLOCK = 2 * NX


def split(value):
    high = value.astype(BF16)
    return high, (value - high.astype(F32)).astype(BF16)


def dot(left, right):
    return jnp.dot(left, right, preferred_element_type=F32)


def lane_broadcast(value, lane):
    return jnp.broadcast_to(value[:, lane : lane + 1], value.shape)


def row_broadcast(value, row):
    return jnp.broadcast_to(value[row : row + 1, :], value.shape)


def eliminate(tiles, begin, end):
    lane = lax.broadcasted_iota(jnp.int32, (8, K), 1)
    sub = lax.broadcasted_iota(jnp.int32, (8, K), 0)
    tiles = list(tiles)
    for b in range(begin, end):
        cur = tiles[b]
        inside = (lane >= 8 * b) & (lane < 8 * b + 8)
        cols = [lane_broadcast(cur, 8 * b + k) for k in range(8)]
        low = {(i, k): row_broadcast(cols[k], i) for k in range(8) for i in range(k, 8)}
        rows = [
            jnp.where(inside, jnp.where(lane == 8 * b + i, 1.0, 0.0), row_broadcast(cur, i))
            for i in range(8)
        ]
        inv = []
        for k in range(8):
            inv.append(lax.rsqrt(low[k, k]))
            for i in range(k + 1, 8):
                low[i, k] = low[i, k] * inv[k]
            for i in range(k + 1, 8):
                for m in range(k + 1, i + 1):
                    low[i, m] = low[i, m] - low[i, k] * low[m, k]
        for k in range(8):
            rows[k] = rows[k] * inv[k]
            for i in range(k + 1, 8):
                rows[i] = rows[i] - low[i, k] * rows[k]
        for t in range(b + 1, len(tiles)):
            col = [lane_broadcast(tiles[t], 8 * b + k) for k in range(8)]
            acc = jnp.where(inside, 0.0, tiles[t])
            for k in range(8):
                col[k] = col[k] * inv[k]
                for m in range(k + 1, 8):
                    col[m] = col[m] - col[k] * low[m, k]
                acc = acc - col[k] * rows[k]
            tiles[t] = acc
        new = rows[0]
        for i in range(1, 8):
            new = jnp.where(sub == i, rows[i], new)
        tiles[b] = jnp.where(lane <= sub + 8 * b, new, 0.0)
    return tiles


def times_transposed(value, inverse):
    left_high, left_low = split(value)
    right_high, right_low = split(inverse.T)
    return dot(left_high, right_high) + (dot(left_high, right_low) + dot(left_low, right_high))


def kernel(
    x_hbm, s_hbm, basis_ref, column_ref, first_ref,
    x_in, s_in, x_high, x_low, s_pair, total, wide, tall,
    zfull,
    core_out, core_in, own, half, in1, part2, in2,
    gram, gram_in, gram_mid, gram_core, gram_z, gram_all, inverse,
    load_sem, core_send, core_recv, s1, r1, s2, r2,
    az_s, az_r, a1_s, a1_r, ac_s, ac_r,
    gx_s, gx_r, gc_s, gc_r, gz_s, gz_r, ga_s, ga_r,
):
    grp, row = lax.axis_index("grp"), lax.axis_index("row")
    x, core = grp // 2, grp % 2
    z, y = row // NY, row % NY
    other = 1 - core
    swap = core == 1
    first = jnp.where(swap, y, x)
    second = jnp.where(swap, x, y)

    def turn(at, step, size):
        return lax.rem(at + step, size)

    def device(px, pc, pz, py):
        return (px * 2 + pc, pz * NY + py)

    def by_axes(at_first, at_second, at_z):
        return device(jnp.where(swap, at_second, at_first), core, at_z, jnp.where(swap, at_first, at_second))

    near = (2, 1, 3)
    ring = (4, 3, 5, 2, 6, 1, 7)
    plane = [(i, j) for i in (2, 1, 3, 0) for j in (2, 1, 3, 0) if i or j]

    def in_plane(step):
        px, py = turn(x, step[0], NX), turn(y, step[1], NY)
        return px * 4 + py, device(px, core, z, py)

    partner = device(x, other, z, y)

    def remote(src, dst, send, recv, to):
        return pltpu.make_async_remote_copy(
            src_ref=src, dst_ref=dst, send_sem=send, recv_sem=recv, device_id=to, device_id_type=MESH
        )

    def arrived(ref, recv):
        remote(ref, ref, recv, recv, partner).wait_recv()

    def sent(ref, send):
        remote(ref, ref, send, send, partner).wait_send()

    loads = []
    for j in range(NBLOCK):
        cols = pl.ds(BLOCK * j, BLOCK)
        pair = (
            pltpu.make_async_copy(s_hbm.at[cols], s_in.at[j], load_sem.at[2 * j]),
            pltpu.make_async_copy(x_hbm.at[:, cols], x_in.at[j], load_sem.at[2 * j + 1]),
        )
        for copy in pair:
            copy.start()
        loads.append(pair)

    barrier = pltpu.get_barrier_semaphore()
    peers = [partner] + [in_plane(s)[1] for s in plane]
    peers += [by_axes(first, turn(second, i, 4), turn(z, k, NZ)) for i in range(4) for k in ring]
    for peer in peers:
        pl.semaphore_signal(barrier, inc=1, device_id=peer, device_id_type=MESH)

    def gram_start(g, block):
        product = jnp.dot(block.T, block, precision=HIGHEST, preferred_element_type=F32)
        gram[g] = product.reshape(16, 8, K)
        for k, s in enumerate(plane):
            at, to = in_plane(s)
            remote(gram.at[g, at], gram_in.at[g, k], gx_s.at[g], gx_r.at[g], to).start()

    def gram_core_step(g):
        arrived(gram_in.at[g], gx_r.at[g])
        tile = gram[g, x * 4 + y]
        for k in range(len(plane)):
            tile = tile + gram_in[g, k]
        gram_mid[g] = tile
        remote(gram_mid.at[g], gram_core.at[g], gc_s.at[g], gc_r.at[g], partner).start()

    def gram_z_step(g):
        arrived(gram_core.at[g], gc_r.at[g])
        gram_z[g, z] = gram_mid[g] + gram_core[g]
        for k in ring:
            to = by_axes(first, second, turn(z, k, NZ))
            remote(gram_z.at[g, z], gram_z.at[g, z], gz_s.at[g], gz_r.at[g], to).start()

    def gram_back_step(g):
        arrived(gram_z.at[g, pl.ds(0, 7)], gz_r.at[g])
        tile = gram_z[g, 0]
        for k in range(1, NZ):
            tile = tile + gram_z[g, k]
        at = x * 4 + y
        gram_all[g, at] = tile
        for s in plane:
            remote(gram_all.at[g, at], gram_all.at[g, at], ga_s.at[g], ga_r.at[g], in_plane(s)[1]).start()

    def gram_arrived(g):
        arrived(gram_all.at[g, pl.ds(0, 15)], ga_r.at[g])

    def factor(g, begin, end):
        source = gram_all if begin == 0 else inverse
        tiles = eliminate([source[g, t] for t in range(16)], begin, end)
        for t in range(16):
            inverse[g, t] = tiles[t]

    def inverse_of(g):
        return inverse[g].reshape(K, K)

    def transposed_block(j):
        part = dot(wide[...], x_high[j])
        part = part[0:K] + part[K : 2 * K] + dot(wide[0:K, :], x_low[j])
        return part.T.reshape(NZ, NY, SLAB, K)

    def prepare(block):
        high, low = split(block.T)
        wide[0:K, :] = high
        wide[K : 2 * K, :] = low

    def core_step(n):
        for px in range(NX):
            core_out[n, px] = transposed_block(px * 2 + other)
            remote(core_out.at[n, px], core_in.at[n, px], core_send.at[n, px], core_recv.at[n, px], partner).start()
        for px in range(NX):
            own[px] = transposed_block(px * 2 + core)

    def first_step(n):
        for px in range(NX):
            arrived(core_in.at[n, px], core_recv.at[n, px])
        for i, away in enumerate((2, 1, 3, 0)):
            at_second = turn(second, away, 4)
            for k, step in enumerate((2, 1, 3, 0)):
                at_first = turn(first, step, 4)
                px = jnp.where(swap, at_second, at_first)
                py = jnp.where(swap, at_first, at_second)
                half[n, i, k] = own[px, :, py] + core_in[n, px, :, py]
                if step:
                    to = by_axes(at_first, second, z)
                    remote(half.at[n, i, k], in1.at[n, i, k], s1.at[n], r1.at[n, i], to).start()

    def second_step(n, i):
        arrived(in1.at[n, i], r1.at[n, i])
        part2[n, i] = (half[n, i, 3] + in1[n, i, 0]) + (in1[n, i, 1] + in1[n, i, 2])
        at_second = turn(second, (2, 1, 3, 0)[i], 4)
        for k, step in enumerate(ring + (0,) if i < 3 else ring):
            at = turn(z, step, NZ)
            to = by_axes(first, at_second, at)
            remote(part2.at[n, i, at], in2.at[n, i * 8 + k], s2.at[n], r2.at[n], to).start()

    def slab_of(n):
        arrived(in2.at[n], r2.at[n])
        sums = [part2[n, 3, z]] + [in2[n, k] for k in range(31)]
        while len(sums) > 1:
            sums = [p + q for p, q in zip(sums[0::2], sums[1::2])]
        return sums[0]

    total[...] = jnp.zeros_like(total)
    for j in range(NBLOCK):
        for copy in loads[j]:
            copy.wait()
        s_high, s_low = split(s_in[j])
        s_pair[j, :, 0:K] = s_high
        s_pair[j, :, K : 2 * K] = s_low
        high, low = split(x_in[j])
        x_high[j] = high
        x_low[j] = low
        part = dot(high, s_pair[j])
        total[...] += part[:, 0:K] + part[:, K : 2 * K] + dot(low, s_high)
    image = total[...]
    prepare(image)
    pl.semaphore_wait(barrier, len(peers))

    gram_start(0, image)
    core_step(0)
    first_step(0)
    gram_core_step(0)
    gram_z_step(0)
    second_step(0, 0)
    second_step(0, 1)
    gram_back_step(0)
    second_step(0, 2)
    second_step(0, 3)
    slab = slab_of(0)

    zfull[core, first, second, z] = slab
    for away in (0, 1, 3, 2):
        for step in ring + (0,) if away else ring:
            to = by_axes(first, turn(second, away, 4), turn(z, step, NZ))
            mine = zfull.at[core, first, second, z]
            remote(mine, mine, az_s.at[0], az_r.at[away], to).start()
    gram_arrived(0)
    factor(0, 0, 7)
    for away in (0, 1, 3, 2):
        at_second = turn(second, 4 - away, 4)
        block = zfull.at[core, first, at_second]
        arrived(block if away else zfull.at[core, first, at_second, pl.ds(0, 7)], az_r.at[away])
        for step in near:
            to = by_axes(turn(first, step, 4), second, z)
            remote(block, block, a1_s.at[0], a1_r.at[away], to).start()
    factor(0, 7, 16)
    for away in (0, 1, 3, 2):
        block = zfull.at[core, :, turn(second, 4 - away, 4)]
        arrived(zfull.at[core, pl.ds(0, 3), 0], a1_r.at[away])
        remote(block, block, ac_s.at[0], ac_r.at[0], partner).start()
    root_rows = math.sqrt(x_hbm.shape[0] * 256)
    first_ref[...] = times_transposed(slab, inverse_of(0)) / root_rows

    def image_of(half_core, px):
        for py in range(NY):
            at_first = jnp.where(half_core == 1, py, px)
            at_second = jnp.where(half_core == 1, px, py)
            high, low = split(zfull[half_core, at_first, at_second])
            tall[px, :, py, :, 0:K] = high
            tall[px, :, py, :, K : 2 * K] = low
        right = tall[px].reshape(BLOCK, 2 * K)
        part = dot(x_high[px * 2 + half_core], right)
        return part[:, 0:K] + part[:, K : 2 * K] + dot(x_low[px * 2 + half_core], right[:, 0:K])

    total[...] = image_of(core, 0)
    for px in range(1, NX):
        total[...] += image_of(core, px)
    arrived(zfull.at[other], ac_r.at[0])
    for px in range(NX):
        total[...] += image_of(other, px)
    total[...] = times_transposed(total[...], inverse_of(0))
    image = total[...]
    prepare(image)

    gram_start(1, image)
    core_step(1)
    first_step(1)
    gram_core_step(1)
    gram_z_step(1)
    second_step(1, 0)
    second_step(1, 1)
    gram_back_step(1)
    second_step(1, 2)
    second_step(1, 3)
    gram_arrived(1)
    factor(1, 0, 16)
    basis_ref[...] = times_transposed(total[...], inverse_of(1)) * root_rows
    column_ref[...] = times_transposed(slab_of(1), inverse_of(1)) / root_rows

    for n in range(2):
        for px in range(NX):
            sent(core_out.at[n, px], core_send.at[n, px])
        sent(in1.at[n], s1.at[n])
        sent(in2.at[n], s2.at[n])
        sent(gram_in.at[n], gx_s.at[n])
        sent(gram_mid.at[n], gc_s.at[n])
        sent(gram_z.at[n, pl.ds(0, 7)], gz_s.at[n])
        sent(gram_all.at[n, pl.ds(0, 15)], ga_s.at[n])
    sent(in2.at[0], az_s.at[0])
    sent(in1.at[0], a1_s.at[0])
    sent(zfull.at[core], ac_s.at[0])


def per_device(embeddings, sketch):
    rows = embeddings.shape[0]
    dma = pltpu.SemaphoreType.DMA
    vmem = pltpu.VMEM
    scratch = [
        vmem((NBLOCK, rows, BLOCK), F32),
        vmem((NBLOCK, BLOCK, K), F32),
        vmem((NBLOCK, rows, BLOCK), BF16),
        vmem((NBLOCK, rows, BLOCK), BF16),
        vmem((NBLOCK, BLOCK, 2 * K), BF16),
        vmem((rows, K), F32),
        vmem((2 * K, rows), BF16),
        vmem((NX, NZ, NY, SLAB, 2 * K), BF16),
        vmem((2, 4, 4, NZ, SLAB, K), F32),
        vmem((2, NX, NZ, NY, SLAB, K), F32),
        vmem((2, NX, NZ, NY, SLAB, K), F32),
        vmem((NX, NZ, NY, SLAB, K), F32),
        vmem((2, 4, 4, NZ, SLAB, K), F32),
        vmem((2, 4, 3, NZ, SLAB, K), F32),
        vmem((2, 4, NZ, SLAB, K), F32),
        vmem((2, 31, SLAB, K), F32),
        vmem((2, 16, 8, K), F32),
        vmem((2, 15, 8, K), F32),
        vmem((2, 8, K), F32),
        vmem((2, 8, K), F32),
        vmem((2, NZ, 8, K), F32),
        vmem((2, 16, 8, K), F32),
        vmem((2, 16, 8, K), F32),
        dma((2 * NBLOCK,)),
        dma((2, NX)), dma((2, NX)),
        dma((2,)), dma((2, 4)),
        dma((2,)), dma((2,)),
        dma((1,)), dma((4,)),
        dma((1,)), dma((4,)),
        dma((1,)), dma((1,)),
        dma((2,)), dma((2,)),
        dma((2,)), dma((2,)),
        dma((2,)), dma((2,)),
        dma((2,)), dma((2,)),
    ]
    return pl.pallas_call(
        kernel,
        name="subspace_iteration",
        out_shape=(
            jax.ShapeDtypeStruct((rows, K), F32),
            jax.ShapeDtypeStruct((SLAB, K), F32),
            jax.ShapeDtypeStruct((SLAB, K), F32),
        ),
        in_specs=[pl.BlockSpec(memory_space=pltpu.HBM)] * 2,
        out_specs=[pl.BlockSpec(memory_space=pltpu.VMEM)] * 3,
        scratch_shapes=scratch,
        compiler_params=pltpu.CompilerParams(
            collective_id=0, has_side_effects=True, vmem_limit_bytes=52 * 2**20
        ),
        cost_estimate=pl.CostEstimate(
            flops=4 * 2 * rows * embeddings.shape[1] * K, bytes_accessed=11 * 2**20, transcendentals=0
        ),
    )(embeddings, sketch)


def solution(mesh):
    rows = P(("grp", "row"), None)
    return jax.shard_map(
        per_device, mesh=mesh, in_specs=(rows, P()), out_specs=(rows, rows, rows), check_vma=False
    )
```

time: 87.3 us -> 71.6 us (0.82)
  Pallas kernels: 83 us -> 69 us
  local copies, waits for them, and re-layouts: 3.49 us -> 1.9 us
    pallas_call x1, Pallas kernels: 83 us -> 69 us  [per_device(): pl.pallas_call(kernel, name='subspace_iteration', out_shape=(jax.ShapeDty...]
    unnamed x5 -> x3, local copies, waits for them, and re-layouts: 3.49 us -> 1.9 us
where the time goes in v2:
time: 71.6 us; the launch traced here: 71.5 us
  Pallas kernels  69 us (96%)
  local copies, waits for them, and re-layouts  1.9 us (3%)
    pallas_call x1, Pallas kernels, per_device(): pl.pallas_call(kernel, name='subspace_iteration', out_shape=(jax.ShapeDty...  69 us
    unnamed x3, local copies, waits for them, and re-layouts  1.9 us

profile of v2, /device:TPU:1, one launch (start us, length us, event | category | flops | bytes accessed | tf_op | source)
XLA Modules:
  0.0 71.5 jit_solution(4498550382204959321)
XLA Ops:
  0.6 69.0 %subspace_iteration.1 = (f32[512,128]{1,0:T(8,128)S(1)}, f32[16,128]{1,0:T(8,128)S(1)}, f32[16,128]{1,0:T(8,128)S(1)}) custom-call(f32[512,4096]{1,0:T(8,128)} %x_hbm.1, f32[4096,128]{1,0:T(8,128)} %s_hbm.1), custom_call_target="tpu_custom_call" | custom-call | flops 2147483648 | bytes 11534336 | tf_op jit(solution)/shard_map/subspace_iteration/pallas_call | solution.py:381
  69.6 0.7 copy.8
  70.3 0.6 copy.9
  70.9 0.6 copy.10

commit v3 on v2

--- a/solution.py
+++ b/solution.py
@@ -34,11 +34,23 @@
     return jnp.broadcast_to(value[row : row + 1, :], value.shape)
 
 
-def eliminate(tiles, begin, end):
+def unit_diagonal(tiles):
+    lane = lax.broadcasted_iota(jnp.int32, (8, K), 1)
+    sub = lax.broadcasted_iota(jnp.int32, (8, K), 0)
+    diagonal = [jnp.where(lane == sub + 8 * t, tile, 0.0) for t, tile in enumerate(tiles)]
+    total = diagonal
+    while len(total) > 1:
+        total = [p + q for p, q in zip(total[0::2], total[1::2])]
+    across = jnp.broadcast_to(lax.rsqrt(jnp.sum(total[0], axis=0, keepdims=True)), (8, K))
+    down = [lax.rsqrt(jnp.broadcast_to(jnp.sum(d, axis=1, keepdims=True), (8, K))) for d in diagonal]
+    return [tile * d * across for tile, d in zip(tiles, down)], across
+
+
+def eliminate(tiles):
     lane = lax.broadcasted_iota(jnp.int32, (8, K), 1)
     sub = lax.broadcasted_iota(jnp.int32, (8, K), 0)
     tiles = list(tiles)
-    for b in range(begin, end):
+    for b in range(len(tiles)):
         cur = tiles[b]
         inside = (lane >= 8 * b) & (lane < 8 * b + 8)
         cols = [lane_broadcast(cur, 8 * b + k) for k in range(8)]
@@ -47,14 +59,18 @@
             jnp.where(inside, jnp.where(lane == 8 * b + i, 1.0, 0.0), row_broadcast(cur, i))
             for i in range(8)
         ]
-        inv = []
-        for k in range(8):
-            inv.append(lax.rsqrt(low[k, k]))
-            for i in range(k + 1, 8):
+        inv = [None] * 8
+        for k in range(0, 8, 2):
+            p, q, r = low[k, k], low[k + 1, k], low[k + 1, k + 1]
+            inv[k] = lax.rsqrt(p)
+            inv[k + 1] = (p * inv[k]) * lax.rsqrt(p * r - q * q)
+            low[k + 1, k] = q * inv[k]
+            for i in range(k + 2, 8):
                 low[i, k] = low[i, k] * inv[k]
-            for i in range(k + 1, 8):
-                for m in range(k + 1, i + 1):
-                    low[i, m] = low[i, m] - low[i, k] * low[m, k]
+                low[i, k + 1] = (low[i, k + 1] - low[i, k] * low[k + 1, k]) * inv[k + 1]
+            for i in range(k + 2, 8):
+                for m in range(k + 2, i + 1):
+                    low[i, m] = (low[i, m] - low[i, k] * low[m, k]) - low[i, k + 1] * low[m, k + 1]
         for k in range(8):
             rows[k] = rows[k] * inv[k]
             for i in range(k + 1, 8):
@@ -109,6 +125,7 @@
         return device(jnp.where(swap, at_second, at_first), core, at_z, jnp.where(swap, at_first, at_second))
 
     near = (2, 1, 3)
+    far_first = near + (0,)
     ring = (4, 3, 5, 2, 6, 1, 7)
     plane = [(i, j) for i in (2, 1, 3, 0) for j in (2, 1, 3, 0) if i or j]
 
@@ -181,11 +198,11 @@
     def gram_arrived(g):
         arrived(gram_all.at[g, pl.ds(0, 15)], ga_r.at[g])
 
-    def factor(g, begin, end):
-        source = gram_all if begin == 0 else inverse
-        tiles = eliminate([source[g, t] for t in range(16)], begin, end)
+    def factor(g):
+        tiles, across = unit_diagonal([gram_all[g, t] for t in range(16)])
+        tiles = eliminate(tiles)
         for t in range(16):
-            inverse[g, t] = tiles[t]
+            inverse[g, t] = tiles[t] * across
 
     def inverse_of(g):
         return inverse[g].reshape(K, K)
@@ -201,30 +218,28 @@
         wide[K : 2 * K, :] = low
 
     def core_step(n):
-        for px in range(NX):
-            core_out[n, px] = transposed_block(px * 2 + other)
-            remote(core_out.at[n, px], core_in.at[n, px], core_send.at[n, px], core_recv.at[n, px], partner).start()
-        for px in range(NX):
-            own[px] = transposed_block(px * 2 + core)
+        for i, step in enumerate(far_first):
+            core_out[n, i] = transposed_block(turn(x, step, NX) * 2 + other)
+            remote(core_out.at[n, i], core_in.at[n, i], core_send.at[n, i], core_recv.at[n, i], partner).start()
 
     def first_step(n):
-        for px in range(NX):
-            arrived(core_in.at[n, px], core_recv.at[n, px])
-        for i, away in enumerate((2, 1, 3, 0)):
-            at_second = turn(second, away, 4)
-            for k, step in enumerate((2, 1, 3, 0)):
-                at_first = turn(first, step, 4)
-                px = jnp.where(swap, at_second, at_first)
-                py = jnp.where(swap, at_first, at_second)
-                half[n, i, k] = own[px, :, py] + core_in[n, px, :, py]
+        for k, step in enumerate(far_first):
+            own[k] = transposed_block(turn(x, step, NX) * 2 + core)
+        for k in range(NX):
+            arrived(core_in.at[n, k], core_recv.at[n, k])
+        for i in range(4):
+            for k, step in enumerate(far_first):
+                xi = jnp.where(swap, i, k)
+                py = turn(y, jnp.where(swap, step, far_first[i]), NY)
+                half[n, i, k] = own[xi, :, py] + core_in[n, xi, :, py]
                 if step:
-                    to = by_axes(at_first, second, z)
+                    to = by_axes(turn(first, step, 4), second, z)
                     remote(half.at[n, i, k], in1.at[n, i, k], s1.at[n], r1.at[n, i], to).start()
 
     def second_step(n, i):
         arrived(in1.at[n, i], r1.at[n, i])
         part2[n, i] = (half[n, i, 3] + in1[n, i, 0]) + (in1[n, i, 1] + in1[n, i, 2])
-        at_second = turn(second, (2, 1, 3, 0)[i], 4)
+        at_second = turn(second, far_first[i], 4)
         for k, step in enumerate(ring + (0,) if i < 3 else ring):
             at = turn(z, step, NZ)
             to = by_axes(first, at_second, at)
@@ -271,8 +286,6 @@
             to = by_axes(first, turn(second, away, 4), turn(z, step, NZ))
             mine = zfull.at[core, first, second, z]
             remote(mine, mine, az_s.at[0], az_r.at[away], to).start()
-    gram_arrived(0)
-    factor(0, 0, 7)
     for away in (0, 1, 3, 2):
         at_second = turn(second, 4 - away, 4)
         block = zfull.at[core, first, at_second]
@@ -280,13 +293,13 @@
         for step in near:
             to = by_axes(turn(first, step, 4), second, z)
             remote(block, block, a1_s.at[0], a1_r.at[away], to).start()
-    factor(0, 7, 16)
+    gram_arrived(0)
+    factor(0)
     for away in (0, 1, 3, 2):
         block = zfull.at[core, :, turn(second, 4 - away, 4)]
         arrived(zfull.at[core, pl.ds(0, 3), 0], a1_r.at[away])
         remote(block, block, ac_s.at[0], ac_r.at[0], partner).start()
     root_rows = math.sqrt(x_hbm.shape[0] * 256)
-    first_ref[...] = times_transposed(slab, inverse_of(0)) / root_rows
 
     def image_of(half_core, px):
         for py in range(NY):
@@ -319,8 +332,9 @@
     gram_back_step(1)
     second_step(1, 2)
     second_step(1, 3)
+    first_ref[...] = times_transposed(slab, inverse_of(0)) / root_rows
     gram_arrived(1)
-    factor(1, 0, 16)
+    factor(1)
     basis_ref[...] = times_transposed(total[...], inverse_of(1)) * root_rows
     column_ref[...] = times_transposed(slab_of(1), inverse_of(1)) / root_rows
 
@@ -336,6 +350,17 @@
     sent(in2.at[0], az_s.at[0])
     sent(in1.at[0], a1_s.at[0])
     sent(zfull.at[core], ac_s.at[0])
+
+
+def hand_over(a, b, c, a_out, b_out, c_out, sem):
+    copies = [
+        pltpu.make_async_copy(src, dst, sem.at[k])
+        for k, (src, dst) in enumerate(((a, a_out), (b, b_out), (c, c_out)))
+    ]
+    for copy in copies:
+        copy.start()
+    for copy in copies:
+        copy.wait()
 
 
 def per_device(embeddings, sketch):
@@ -378,7 +403,7 @@
         dma((2,)), dma((2,)),
         dma((2,)), dma((2,)),
     ]
-    return pl.pallas_call(
+    results = pl.pallas_call(
         kernel,
         name="subspace_iteration",
         out_shape=(
@@ -396,6 +421,15 @@
             flops=4 * 2 * rows * embeddings.shape[1] * K, bytes_accessed=11 * 2**20, transcendentals=0
         ),
     )(embeddings, sketch)
+    return pl.pallas_call(
+        hand_over,
+        name="hand_over",
+        out_shape=tuple(jax.ShapeDtypeStruct(r.shape, r.dtype) for r in results),
+        in_specs=[pl.BlockSpec(memory_space=pl.ANY)] * 3,
+        out_specs=[pl.BlockSpec(memory_space=pl.ANY)] * 3,
+        scratch_shapes=[dma((3,))],
+        compiler_params=pltpu.CompilerParams(vmem_limit_bytes=2**20),
+    )(*results)
 
 
 def solution(mesh):

time: 71.6 us -> 69.7 us (0.973)
  local copies, waits for them, and re-layouts: 1.9 us -> 0 us
    unnamed x3 -> x0, local copies, waits for them, and re-layouts: 1.9 us -> none
    pallas_call x1, Pallas kernels: 69 us -> 68.1 us  [per_device(): pl.pallas_call(kernel, name='subspace_iteration', out_shape=(jax.ShapeDty...]
    pallas_call x0 -> x1, Pallas kernels: none -> 0.74 us  [per_device(): pl.pallas_call(hand_over, name='hand_over', out_shape=tuple((jax.ShapeDty...]
where the time goes in v3:
time: 69.7 us
  Pallas kernels  68.9 us (99%)
  between operations  0.8 us (1%)
    pallas_call x1, Pallas kernels, per_device(): pl.pallas_call(kernel, name='subspace_iteration', out_shape=(jax.ShapeDty...  68.1 us

profile of v3, /device:TPU:1, one launch (start us, length us, event | category | flops | bytes accessed | tf_op | source)
XLA Modules:
  0.0 69.7 jit_solution(4682425828594212693)
XLA Ops:
  0.6 68.1 %subspace_iteration.1 = (f32[512,128]{1,0:T(8,128)S(1)}, f32[16,128]{1,0:T(8,128)S(1)}, f32[16,128]{1,0:T(8,128)S(1)}) custom-call(f32[512,4096]{1,0:T(8,128)} %x_hbm.1, f32[4096,128]{1,0:T(8,128)} %s_hbm.1), custom_call_target="tpu_custom_call" | custom-call | flops 2147483648 | bytes 11534336 | tf_op jit(solution)/shard_map/subspace_iteration/pallas_call | solution.py:406
  68.8 0.7 %hand_over.1 = (f32[512,128]{1,0:T(8,128)}, f32[16,128]{1,0:T(8,128)}, f32[16,128]{1,0:T(8,128)}) custom-call(f32[512,128]{1,0:T(8,128)S(1)} %get-tuple-element.6.a, f32[16,128]{1,0:T(8,128)S(1)} %get-tuple-element.7.b, f32[16,128]{1,0:T(8,128)S(1)} %get-tuple-element.8.c), custom_call_target="tpu_custom_call" | custom-call | tf_op jit(solution)/shard_map/hand_over/pallas_call | solution.py:424

commit v4 on v3

--- a/solution.py
+++ b/solution.py
@@ -50,10 +50,10 @@
     lane = lax.broadcasted_iota(jnp.int32, (8, K), 1)
     sub = lax.broadcasted_iota(jnp.int32, (8, K), 0)
     tiles = list(tiles)
+    cols = [lane_broadcast(tiles[0], k) for k in range(8)]
     for b in range(len(tiles)):
         cur = tiles[b]
         inside = (lane >= 8 * b) & (lane < 8 * b + 8)
-        cols = [lane_broadcast(cur, 8 * b + k) for k in range(8)]
         low = {(i, k): row_broadcast(cols[k], i) for k in range(8) for i in range(k, 8)}
         rows = [
             jnp.where(inside, jnp.where(lane == 8 * b + i, 1.0, 0.0), row_broadcast(cur, i))
@@ -77,6 +77,7 @@
                 rows[i] = rows[i] - low[i, k] * rows[k]
         for t in range(b + 1, len(tiles)):
             col = [lane_broadcast(tiles[t], 8 * b + k) for k in range(8)]
+            ahead = [lane_broadcast(tiles[t], 8 * t + k) for k in range(8)] if t == b + 1 else []
             acc = jnp.where(inside, 0.0, tiles[t])
             for k in range(8):
                 col[k] = col[k] * inv[k]
@@ -84,6 +85,10 @@
                     col[m] = col[m] - col[k] * low[m, k]
                 acc = acc - col[k] * rows[k]
             tiles[t] = acc
+            if ahead:
+                for m in range(8):
+                    ahead = [a - col[m] * row_broadcast(col[m], k) for k, a in enumerate(ahead)]
+                cols = ahead
         new = rows[0]
         for i in range(1, 8):
             new = jnp.where(sub == i, rows[i], new)
@@ -91,10 +96,9 @@
     return tiles
 
 
-def times_transposed(value, inverse):
-    left_high, left_low = split(value)
-    right_high, right_low = split(inverse.T)
-    return dot(left_high, right_high) + (dot(left_high, right_low) + dot(left_low, right_high))
+def product(value, right_high, right_low):
+    high, low = split(value)
+    return dot(high, right_high) + (dot(high, right_low) + dot(low, right_high))
 
 
 def kernel(
@@ -201,11 +205,13 @@
     def factor(g):
         tiles, across = unit_diagonal([gram_all[g, t] for t in range(16)])
         tiles = eliminate(tiles)
-        for t in range(16):
-            inverse[g, t] = tiles[t] * across
-
-    def inverse_of(g):
-        return inverse[g].reshape(K, K)
+        whole = jnp.concatenate([tile * across for tile in tiles], axis=0)
+        high, low = split(whole.T)
+        inverse[g, 0] = high
+        inverse[g, 1] = low
+
+    def normalized(value, g):
+        return product(value, inverse[g, 0], inverse[g, 1])
 
     def transposed_block(j):
         part = dot(wide[...], x_high[j])
@@ -318,11 +324,11 @@
     arrived(zfull.at[other], ac_r.at[0])
     for px in range(NX):
         total[...] += image_of(other, px)
-    total[...] = times_transposed(total[...], inverse_of(0))
+    total[...] = normalized(total[...], 0)
     image = total[...]
+
+    gram_start(1, image)
     prepare(image)
-
-    gram_start(1, image)
     core_step(1)
     first_step(1)
     gram_core_step(1)
@@ -332,11 +338,11 @@
     gram_back_step(1)
     second_step(1, 2)
     second_step(1, 3)
-    first_ref[...] = times_transposed(slab, inverse_of(0)) / root_rows
+    first_ref[...] = normalized(slab, 0) / root_rows
     gram_arrived(1)
     factor(1)
-    basis_ref[...] = times_transposed(total[...], inverse_of(1)) * root_rows
-    column_ref[...] = times_transposed(slab_of(1), inverse_of(1)) / root_rows
+    basis_ref[...] = normalized(total[...], 1) * root_rows
+    column_ref[...] = normalized(slab_of(1), 1) / root_rows
 
     for n in range(2):
         for px in range(NX):
@@ -390,7 +396,7 @@
         vmem((2, 8, K), F32),
         vmem((2, NZ, 8, K), F32),
         vmem((2, 16, 8, K), F32),
-        vmem((2, 16, 8, K), F32),
+        vmem((2, 2, K, K), BF16),
         dma((2 * NBLOCK,)),
         dma((2, NX)), dma((2, NX)),
         dma((2,)), dma((2, 4)),

time: 69.7 us -> 68.3 us (0.980)
  Pallas kernels: 68.9 us -> 67.5 us
    pallas_call x1, Pallas kernels: 68.1 us -> 66.7 us  [per_device(): pl.pallas_call(kernel, name='subspace_iteration', out_shape=(jax.ShapeDty...]
where the time goes in v4:
time: 68.3 us; the launch traced here: 68.2 us
  Pallas kernels  67.5 us (99%)
  between operations  0.8 us (1%)
    pallas_call x1, Pallas kernels, per_device(): pl.pallas_call(kernel, name='subspace_iteration', out_shape=(jax.ShapeDty...  66.7 us

profile of v4, /device:TPU:1, one launch (start us, length us, event | category | flops | bytes accessed | tf_op | source)
XLA Modules:
  0.0 68.2 jit_solution(4602189084367894321)
XLA Ops:
  0.6 66.7 %subspace_iteration.1 = (f32[512,128]{1,0:T(8,128)S(1)}, f32[16,128]{1,0:T(8,128)S(1)}, f32[16,128]{1,0:T(8,128)S(1)}) custom-call(f32[512,4096]{1,0:T(8,128)} %x_hbm.1, f32[4096,128]{1,0:T(8,128)} %s_hbm.1), custom_call_target="tpu_custom_call" | custom-call | flops 2147483648 | bytes 11534336 | tf_op jit(solution)/shard_map/subspace_iteration/pallas_call | solution.py:412
  67.4 0.7 %hand_over.1 = (f32[512,128]{1,0:T(8,128)}, f32[16,128]{1,0:T(8,128)}, f32[16,128]{1,0:T(8,128)}) custom-call(f32[512,128]{1,0:T(8,128)S(1)} %get-tuple-element.6.a, f32[16,128]{1,0:T(8,128)S(1)} %get-tuple-element.7.b, f32[16,128]{1,0:T(8,128)S(1)} %get-tuple-element.8.c), custom_call_target="tpu_custom_call" | custom-call | tf_op jit(solution)/shard_map/hand_over/pallas_call | solution.py:430

commit v5 on v4

--- a/solution.py
+++ b/solution.py
@@ -34,14 +34,17 @@
     return jnp.broadcast_to(value[row : row + 1, :], value.shape)
 
 
+def tree_sum(terms):
+    while len(terms) > 1:
+        terms = [p + q for p, q in zip(terms[0::2], terms[1::2])]
+    return terms[0]
+
+
 def unit_diagonal(tiles):
     lane = lax.broadcasted_iota(jnp.int32, (8, K), 1)
     sub = lax.broadcasted_iota(jnp.int32, (8, K), 0)
     diagonal = [jnp.where(lane == sub + 8 * t, tile, 0.0) for t, tile in enumerate(tiles)]
-    total = diagonal
-    while len(total) > 1:
-        total = [p + q for p, q in zip(total[0::2], total[1::2])]
-    across = jnp.broadcast_to(lax.rsqrt(jnp.sum(total[0], axis=0, keepdims=True)), (8, K))
+    across = jnp.broadcast_to(lax.rsqrt(jnp.sum(tree_sum(diagonal), axis=0, keepdims=True)), (8, K))
     down = [lax.rsqrt(jnp.broadcast_to(jnp.sum(d, axis=1, keepdims=True), (8, K))) for d in diagonal]
     return [tile * d * across for tile, d in zip(tiles, down)], across
 
@@ -106,10 +109,10 @@
     x_in, s_in, x_high, x_low, s_pair, total, wide, tall,
     zfull,
     core_out, core_in, own, half, in1, part2, in2,
-    gram, gram_in, gram_mid, gram_core, gram_z, gram_all, inverse,
+    gram, gram_in, gram_z, gram_all, inverse,
     load_sem, core_send, core_recv, s1, r1, s2, r2,
     az_s, az_r, a1_s, a1_r, ac_s, ac_r,
-    gx_s, gx_r, gc_s, gc_r, gz_s, gz_r, ga_s, ga_r,
+    gx_s, gx_r, gz_s, gz_r, ga_s, ga_r,
 ):
     grp, row = lax.axis_index("grp"), lax.axis_index("row")
     x, core = grp // 2, grp % 2
@@ -138,6 +141,7 @@
         return px * 4 + py, device(px, core, z, py)
 
     partner = device(x, other, z, y)
+    column = [device(x, c, turn(z, k, NZ), y) for k in ring for c in (core, other)] + [partner]
 
     def remote(src, dst, send, recv, to):
         return pltpu.make_async_remote_copy(
@@ -164,6 +168,7 @@
     barrier = pltpu.get_barrier_semaphore()
     peers = [partner] + [in_plane(s)[1] for s in plane]
     peers += [by_axes(first, turn(second, i, 4), turn(z, k, NZ)) for i in range(4) for k in ring]
+    peers += [device(x, other, turn(z, k, NZ), y) for k in ring]
     for peer in peers:
         pl.semaphore_signal(barrier, inc=1, device_id=peer, device_id_type=MESH)
 
@@ -174,26 +179,16 @@
             at, to = in_plane(s)
             remote(gram.at[g, at], gram_in.at[g, k], gx_s.at[g], gx_r.at[g], to).start()
 
-    def gram_core_step(g):
+    def gram_z_step(g):
         arrived(gram_in.at[g], gx_r.at[g])
-        tile = gram[g, x * 4 + y]
-        for k in range(len(plane)):
-            tile = tile + gram_in[g, k]
-        gram_mid[g] = tile
-        remote(gram_mid.at[g], gram_core.at[g], gc_s.at[g], gc_r.at[g], partner).start()
-
-    def gram_z_step(g):
-        arrived(gram_core.at[g], gc_r.at[g])
-        gram_z[g, z] = gram_mid[g] + gram_core[g]
-        for k in ring:
-            to = by_axes(first, second, turn(z, k, NZ))
-            remote(gram_z.at[g, z], gram_z.at[g, z], gz_s.at[g], gz_r.at[g], to).start()
+        at = core * NZ + z
+        gram_z[g, at] = tree_sum([gram[g, x * 4 + y]] + [gram_in[g, k] for k in range(15)])
+        for to in column:
+            remote(gram_z.at[g, at], gram_z.at[g, at], gz_s.at[g], gz_r.at[g], to).start()
 
     def gram_back_step(g):
-        arrived(gram_z.at[g, pl.ds(0, 7)], gz_r.at[g])
-        tile = gram_z[g, 0]
-        for k in range(1, NZ):
-            tile = tile + gram_z[g, k]
+        arrived(gram_z.at[g, pl.ds(0, 15)], gz_r.at[g])
+        tile = tree_sum([gram_z[g, k] for k in range(16)])
         at = x * 4 + y
         gram_all[g, at] = tile
         for s in plane:
@@ -253,10 +248,7 @@
 
     def slab_of(n):
         arrived(in2.at[n], r2.at[n])
-        sums = [part2[n, 3, z]] + [in2[n, k] for k in range(31)]
-        while len(sums) > 1:
-            sums = [p + q for p, q in zip(sums[0::2], sums[1::2])]
-        return sums[0]
+        return tree_sum([part2[n, 3, z]] + [in2[n, k] for k in range(31)])
 
     total[...] = jnp.zeros_like(total)
     for j in range(NBLOCK):
@@ -277,7 +269,6 @@
     gram_start(0, image)
     core_step(0)
     first_step(0)
-    gram_core_step(0)
     gram_z_step(0)
     second_step(0, 0)
     second_step(0, 1)
@@ -331,7 +322,6 @@
     prepare(image)
     core_step(1)
     first_step(1)
-    gram_core_step(1)
     gram_z_step(1)
     second_step(1, 0)
     second_step(1, 1)
@@ -350,8 +340,7 @@
         sent(in1.at[n], s1.at[n])
         sent(in2.at[n], s2.at[n])
         sent(gram_in.at[n], gx_s.at[n])
-        sent(gram_mid.at[n], gc_s.at[n])
-        sent(gram_z.at[n, pl.ds(0, 7)], gz_s.at[n])
+        sent(gram_z.at[n, pl.ds(0, 15)], gz_s.at[n])
         sent(gram_all.at[n, pl.ds(0, 15)], ga_s.at[n])
     sent(in2.at[0], az_s.at[0])
     sent(in1.at[0], a1_s.at[0])
@@ -392,9 +381,7 @@
         vmem((2, 31, SLAB, K), F32),
         vmem((2, 16, 8, K), F32),
         vmem((2, 15, 8, K), F32),
-        vmem((2, 8, K), F32),
-        vmem((2, 8, K), F32),
-        vmem((2, NZ, 8, K), F32),
+        vmem((2, 2 * NZ, 8, K), F32),
         vmem((2, 16, 8, K), F32),
         vmem((2, 2, K, K), BF16),
         dma((2 * NBLOCK,)),
@@ -404,7 +391,6 @@
         dma((1,)), dma((4,)),
         dma((1,)), dma((4,)),
         dma((1,)), dma((1,)),
-        dma((2,)), dma((2,)),
         dma((2,)), dma((2,)),
         dma((2,)), dma((2,)),
         dma((2,)), dma((2,)),

time: 68.3 us -> 68 us (level)
  no operation moved by 1% of the time
where the time goes in v5:
time: 68 us; the launch traced here: 67.9 us
  Pallas kernels  67.1 us (99%)
  between operations  0.8 us (1%)
    pallas_call x1, Pallas kernels, per_device(): pl.pallas_call(kernel, name='subspace_iteration', out_shape=(jax.ShapeDty...  66.4 us

profile of v5, /device:TPU:1, one launch (start us, length us, event | category | flops | bytes accessed | tf_op | source)
XLA Modules:
  0.0 67.9 jit_solution(7420517715167747303)
XLA Ops:
  0.6 66.4 %subspace_iteration.1 = (f32[512,128]{1,0:T(8,128)S(1)}, f32[16,128]{1,0:T(8,128)S(1)}, f32[16,128]{1,0:T(8,128)S(1)}) custom-call(f32[512,4096]{1,0:T(8,128)} %x_hbm.1, f32[4096,128]{1,0:T(8,128)} %s_hbm.1), custom_call_target="tpu_custom_call" | custom-call | flops 2147483648 | bytes 11534336 | tf_op jit(solution)/shard_map/subspace_iteration/pallas_call | solution.py:398
  67.0 0.7 %hand_over.1 = (f32[512,128]{1,0:T(8,128)}, f32[16,128]{1,0:T(8,128)}, f32[16,128]{1,0:T(8,128)}) custom-call(f32[512,128]{1,0:T(8,128)S(1)} %get-tuple-element.6.a, f32[16,128]{1,0:T(8,128)S(1)} %get-tuple-element.7.b, f32[16,128]{1,0:T(8,128)S(1)} %get-tuple-element.8.c), custom_call_target="tpu_custom_call" | custom-call | tf_op jit(solution)/shard_map/hand_over/pallas_call | solution.py:416
